TPU v7x, 32 devices: a whole 2x2x4 slice. The times are simulated.
32 devices in a mesh: row: 8 (over y, x, core), ctr: 4 (over z).
Axes of the slice: x: 2, y: 2, z: 4, core: 2. Of those that a mesh axis runs over, the one named last changes fastest.
Arguments:
- left_factor: bfloat16 [32, 1024, 1024], P('row', None, 'ctr'), may hold values from -6 to 6
- left_inner: bfloat16 [32, 1024, 1024], P('row', None, 'ctr'), may hold values from -0.1875 to 0.1875
- right_inner: bfloat16 [1024, 1024], P('row', 'ctr'), may hold values from -6 to 6
- right_outer: bfloat16 [1024, 1024], P('row', 'ctr'), may hold values from -0.03125 to 0.03125
- pattern: int32 [32, 32], P('row', 'ctr'), may hold values from 0 to 1, as said below
- start_matrix: int32 [1024, 32], replicated, may hold values from -4 to 4
Outputs:
- compressed_left: bfloat16 [32, 1024, 32], P('row')
- compressed_right: bfloat16 [32, 1024, 32], P('row')
Inputs may be any that keep to these rules, and one draw needn't show every extreme that they name: `pattern`: in every tile row at least one of each aligned group of four contraction tiles is kept; how many are kept differs from row to row.
All inputs are finite; a program needn't handle non-finite values.
Results may differ from a plain program's by a relative error of at most 0.025.
Values may be sent and summed in bfloat16 or wider, within the bound.
A program may use at most 64 MiB of HBM per device.

v0:
```python
import math

import jax
import jax.numpy as jnp
from jax import lax
from jax.sharding import PartitionSpec as P

STEPS = 2


highest = lax.Precision.HIGHEST


def gram_of(panel):
    return jnp.einsum(
        "itr,its->irs", panel, panel, precision=highest, preferred_element_type=jnp.float32
    )


def solve_rows(gram_matrix, panel):
    factor_low = jnp.linalg.cholesky(gram_matrix)
    return lax.linalg.triangular_solve(
        factor_low, panel, left_side=False, lower=True, transpose_a=True
    )


def reduced_basis(partial_value):
    summed = lax.psum(partial_value.astype(jnp.bfloat16), "ctr").astype(jnp.float32)
    return solve_rows(gram_of(summed), summed).astype(jnp.bfloat16)


def reduced_weights(partial_value):
    return lax.psum(partial_value.astype(jnp.bfloat16), "ctr")


def local(left_factor, left_inner, right_inner, right_outer, pattern, start_matrix):
    rows_here = left_factor.shape[0]
    tile_len = left_factor.shape[1]
    columns_here = left_factor.shape[2]
    rank_len = start_matrix.shape[1]
    blocks = columns_here // rank_len
    inner_piece = lax.all_gather(right_inner, "row", axis=0, tiled=True)
    outer_piece = lax.all_gather(right_outer, "row", axis=0, tiled=True)
    taken = inner_piece.shape[0]
    coupled = jnp.einsum(
        "itkr,tks->ikrs",
        left_inner.reshape(rows_here, taken, blocks, rank_len),
        inner_piece.reshape(taken, blocks, rank_len),
        preferred_element_type=jnp.float32,
    )
    coupled, outer_full = (coupled, outer_piece)
    coupled = (coupled * pattern.astype(jnp.float32)[:, :, None, None]).astype(jnp.bfloat16)
    inner_block = lax.optimization_barrier(coupled).astype(jnp.float32)

    def forward(vectors):
        shrunk = jnp.einsum(
            "tc,itq->icq", outer_full, vectors, preferred_element_type=jnp.float32
        ).reshape(rows_here, blocks, rank_len, rank_len)
        mapped = jnp.einsum("ikrs,iksq->ikrq", inner_block, shrunk, precision=highest)
        mapped = mapped.astype(jnp.bfloat16).reshape(rows_here, columns_here, rank_len)
        return jnp.einsum("itc,icq->itq", left_factor, mapped, preferred_element_type=jnp.float32)

    def adjoint(vectors):
        shrunk = jnp.einsum(
            "itc,itq->icq", left_factor, vectors, preferred_element_type=jnp.float32
        ).reshape(rows_here, blocks, rank_len, rank_len)
        mapped = jnp.einsum("ikrs,ikrq->iksq", inner_block, shrunk, precision=highest)
        mapped = mapped.astype(jnp.bfloat16).reshape(rows_here, columns_here, rank_len)
        return jnp.einsum("tc,icq->itq", outer_full, mapped, preferred_element_type=jnp.float32)

    start_bf = jnp.broadcast_to(
        start_matrix.astype(jnp.bfloat16)[None], (rows_here, tile_len, rank_len)
    )
    basis_now = reduced_basis(forward(start_bf))
    for sweep_index in range(STEPS):
        dual_basis = reduced_basis(adjoint(basis_now))
        basis_now = reduced_basis(forward(dual_basis))
    weights = reduced_weights(adjoint(basis_now))
    compressed_left = (basis_now.astype(jnp.float32) * math.sqrt(tile_len)).astype(jnp.bfloat16)
    return (compressed_left, weights)


def solution(mesh):
    return jax.shard_map(
        local,
        mesh=mesh,
        in_specs=(
            P("row", None, "ctr"),
            P("row", None, "ctr"),
            P("row", "ctr"),
            P("row", "ctr"),
            P("row", "ctr"),
            P(),
        ),
        out_specs=(P("row", None, None), P("row", None, None)),
        check_vma=False,
    )
```

profile of v0, /device:TPU:0, one launch (start us, length us, event | category | flops | bytes accessed | tf_op | source)
XLA Modules:
  0.0 395.0 jit_solution(3704827438082336699)
XLA Ops:
  7.2 4.1 %copy.64 = bf16[4,1024,256]{1,2,0:T(8,128)(2,1)} copy(bf16[4,1024,256]{2,1,0:T(8,128)(2,1)} %param.10) | data formatting | bytes 4194304 | tf_op args[1]
  11.4 11.3 %all_gather.6 = bf16[1024,256]{1,0:T(8,128)(2,1)S(1)} all-gather(bf16[128,256]{1,0:T(8,128)(2,1)S(1)} %copy-done.2), channel_id=1, replica_groups=mesh['row'=8,'ctr'=4] {'row'}, dimensions={0}, use_global_device_ids=true | all-gather | bytes 589824 | tf_op jit(solution)/shard_map/all_gather | solution.py:42
  23.0 3.4 fusion.13
  26.4 9.8 %all_gather.7 = bf16[1024,256]{1,0:T(8,128)(2,1)S(1)} all-gather(bf16[128,256]{1,0:T(8,128)(2,1)S(1)} %copy-done.3), channel_id=1, replica_groups=mesh['row'=8,'ctr'=4] {'row'}, dimensions={0}, use_global_device_ids=true | all-gather | bytes 589824 | tf_op jit(solution)/shard_map/all_gather | solution.py:43
  38.7 35.7 %all-reduce.7.cloned.1.call-done = bf16[4,1024,32]{1,2,0:T(8,128)(2,1)} async-done(((bf16[4,1024,32]{1,2,0:T(8,128)(2,1)}), bf16[4,1024,32]{1,2,0:T(8,128)(2,1)}) %all-reduce.7.cloned.1.call-update) | async-done | bytes 262160 | tf_op jit(solution)/shard_map/psum | solution.py:28
  75.8 11.7 %custom-call.14 = f32[4,32,32]{2,1,0:T(8,128)S(1)} custom-call(f32[4,32,32]{2,1,0:T(8,128)S(1)} %fusion.49), custom_call_target="Cholesky" | custom-call | tf_op jit(solution)/shard_map/jit(cholesky)/cholesky | solution.py:21
  87.7 9.8 %custom-call.15 = f32[4,1,32,32]{2,3,1,0:T(8,128)S(1)} custom-call(f32[4,1,32,32]{3,2,1,0:T(8,128)S(1)} %select_bitcast_fusion.4), custom_call_target="InvertDiagBlocksLowerTriangular" | custom-call | tf_op jit(solution)/shard_map/triangular_solve/custom-call.0 | solution.py:22
  97.6 1.6 fusion.8
  101.5 35.2 %all-reduce.9.cloned.1.call-done = bf16[4,1024,32]{1,2,0:T(8,128)(2,1)} async-done(((bf16[4,1024,32]{1,2,0:T(8,128)(2,1)}), bf16[4,1024,32]{1,2,0:T(8,128)(2,1)}) %all-reduce.9.cloned.1.call-update) | async-done | bytes 262160 | tf_op jit(solution)/shard_map/psum | solution.py:28
  138.0 11.7 %custom-call.16 = f32[4,32,32]{2,1,0:T(8,128)S(1)} custom-call(f32[4,32,32]{2,1,0:T(8,128)S(1)} %fusion.47), custom_call_target="Cholesky" | custom-call | tf_op jit(solution)/shard_map/jit(cholesky)/cholesky | solution.py:21
  149.9 9.8 %custom-call.17 = f32[4,1,32,32]{2,3,1,0:T(8,128)S(1)} custom-call(f32[4,1,32,32]{3,2,1,0:T(8,128)S(1)} %select_bitcast_fusion.3), custom_call_target="InvertDiagBlocksLowerTriangular" | custom-call | tf_op jit(solution)/shard_map/triangular_solve/custom-call.0 | solution.py:22
  159.8 1.6 fusion.9
  163.8 35.2 %all-reduce.11.cloned.1.call-done = bf16[4,1024,32]{1,2,0:T(8,128)(2,1)} async-done(((bf16[4,1024,32]{1,2,0:T(8,128)(2,1)}), bf16[4,1024,32]{1,2,0:T(8,128)(2,1)}) %all-reduce.11.cloned.1.call-update) | async-done | bytes 262160 | tf_op jit(solution)/shard_map/psum | solution.py:28
  200.3 11.7 %custom-call.18 = f32[4,32,32]{2,1,0:T(8,128)S(1)} custom-call(f32[4,32,32]{2,1,0:T(8,128)S(1)} %fusion.45), custom_call_target="Cholesky" | custom-call | tf_op jit(solution)/shard_map/jit(cholesky)/cholesky | solution.py:21
  212.3 9.8 %custom-call.19 = f32[4,1,32,32]{2,3,1,0:T(8,128)S(1)} custom-call(f32[4,1,32,32]{3,2,1,0:T(8,128)S(1)} %select_bitcast_fusion.2), custom_call_target="InvertDiagBlocksLowerTriangular" | custom-call | tf_op jit(solution)/shard_map/triangular_solve/custom-call.0 | solution.py:22
  226.2 35.0 %all-reduce.13.cloned.1.call-done = bf16[4,1024,32]{1,2,0:T(8,128)(2,1)} async-done(((bf16[4,1024,32]{1,2,0:T(8,128)(2,1)}), bf16[4,1024,32]{1,2,0:T(8,128)(2,1)}) %all-reduce.13.cloned.1.call-update) | async-done | bytes 262160 | tf_op jit(solution)/shard_map/psum | solution.py:28
  262.5 11.7 %custom-call.20 = f32[4,32,32]{2,1,0:T(8,128)S(1)} custom-call(f32[4,32,32]{2,1,0:T(8,128)S(1)} %fusion.43), custom_call_target="Cholesky" | custom-call | tf_op jit(solution)/shard_map/jit(cholesky)/cholesky | solution.py:21
  274.5 9.8 %custom-call.21 = f32[4,1,32,32]{2,3,1,0:T(8,128)S(1)} custom-call(f32[4,1,32,32]{3,2,1,0:T(8,128)S(1)} %select_bitcast_fusion.1), custom_call_target="InvertDiagBlocksLowerTriangular" | custom-call | tf_op jit(solution)/shard_map/triangular_solve/custom-call.0 | solution.py:22
  288.4 35.2 %all-reduce.15.cloned.1.call-done = bf16[4,1024,32]{1,2,0:T(8,128)(2,1)} async-done(((bf16[4,1024,32]{1,2,0:T(8,128)(2,1)}), bf16[4,1024,32]{1,2,0:T(8,128)(2,1)}) %all-reduce.15.cloned.1.call-update) | async-done | bytes 262160 | tf_op jit(solution)/shard_map/psum | solution.py:28
  324.9 11.7 %custom-call.22 = f32[4,32,32]{2,1,0:T(8,128)S(1)} custom-call(f32[4,32,32]{2,1,0:T(8,128)S(1)} %fusion.41), custom_call_target="Cholesky" | custom-call | tf_op jit(solution)/shard_map/jit(cholesky)/cholesky | solution.py:21
  336.8 9.8 %custom-call.23 = f32[4,1,32,32]{2,3,1,0:T(8,128)S(1)} custom-call(f32[4,1,32,32]{3,2,1,0:T(8,128)S(1)} %select_bitcast_fusion), custom_call_target="InvertDiagBlocksLowerTriangular" | custom-call | tf_op jit(solution)/shard_map/triangular_solve/custom-call.0 | solution.py:22
  346.7 2.3 multiply_convert_fusion
  351.2 35.2 %all-reduce.17.cloned.1.call-done = bf16[4,1024,32]{1,2,0:T(8,128)(2,1)} async-done(((bf16[4,1024,32]{1,2,0:T(8,128)(2,1)}), bf16[4,1024,32]{1,2,0:T(8,128)(2,1)}) %all-reduce.17.cloned.1.call-update) | async-done | bytes 262160 | tf_op jit(solution)/shard_map/psum | solution.py:33
  386.4 1.7 copy.145
  (84 shorter events, 25.5 us)
Async XLA Ops:
  7.2 30.0 %copy-start = (bf16[4,1024,256]{2,1,0:T(8,128)(2,1)S(1)}, bf16[4,1024,256]{2,1,0:T(8,128)(2,1)}, u32[]{:S(2)}) copy-start(bf16[4,1024,256]{2,1,0:T(8,128)(2,1)} %param.9) | copy-start | bytes 6291460
  7.2 4.2 %copy-start.2 = (bf16[128,256]{1,0:T(8,128)(2,1)S(1)}, bf16[128,256]{1,0:T(8,128)(2,1)}, u32[]{:S(2)}) copy-start(bf16[128,256]{1,0:T(8,128)(2,1)} %param.11) | copy-start | bytes 196612
  7.2 15.7 %copy-start.4 = (s32[4,8]{1,0:T(4,128)S(1)}, s32[4,8]{1,0:T(4,128)}, u32[]{:S(2)}) copy-start(s32[4,8]{1,0:T(4,128)} %param.13) | copy-start | bytes 388
  7.2 67.2 %all-reduce.7.cloned.1.call-start = ((), (), s32[]{:S(2)}) async-start(), calls=%async_computation | async-start | bytes 524288 | tf_op jit(solution)/shard_map/psum | solution.py:28
  22.7 3.7 copy-start.3
  23.0 13.2 %copy-start.1 = (s32[1024,32]{0,1:T(8,128)S(1)}, s32[1024,32]{0,1:T(8,128)}, u32[]{:S(2)}) copy-start(s32[1024,32]{0,1:T(8,128)} %param.14) | copy-start | bytes 393220
  38.6 98.0 %all-reduce.9.cloned.1.call-start = ((), (), s32[]{:S(2)}) async-start(), calls=%async_computation.1 | async-start | bytes 524288 | tf_op jit(solution)/shard_map/psum | solution.py:28
  101.4 97.6 %all-reduce.11.cloned.1.call-start = ((), (), s32[]{:S(2)}) async-start(), calls=%async_computation.2 | async-start | bytes 524288 | tf_op jit(solution)/shard_map/psum | solution.py:28
  163.7 97.5 %all-reduce.13.cloned.1.call-start = ((), (), s32[]{:S(2)}) async-start(), calls=%async_computation.3 | async-start | bytes 524288 | tf_op jit(solution)/shard_map/psum | solution.py:28
  226.0 97.5 %all-reduce.15.cloned.1.call-start = ((), (), s32[]{:S(2)}) async-start(), calls=%async_computation.4 | async-start | bytes 524288 | tf_op jit(solution)/shard_map/psum | solution.py:28
  288.3 98.1 %all-reduce.17.cloned.1.call-start = ((), (), s32[]{:S(2)}) async-start(), calls=%async_computation.5 | async-start | bytes 524288 | tf_op jit(solution)/shard_map/psum | solution.py:33
Sparse Core Ops, SparseCore 0:
  38.7 35.6 all-reduce.6
  101.5 35.0 all-reduce.8
  163.9 35.0 all-reduce.10
  226.1 35.0 all-reduce.12
  288.4 35.0 all-reduce.14
  351.3 35.0 all-reduce.16
where the time goes:
time: 395 us
  waiting for transfers between devices  212 us (54%)
  other arithmetic  109 us (28%)
  matrix products  30.5 us (8%)
  blocking collectives  21.1 us (5%)
  between operations  14.4 us (4%)
  local copies, waits for them, and re-layouts  7.79 us (2%)
    psum x5, waiting for transfers between devices, reduced_basis(): lax.psum(partial_value.astype(jnp.bfloat16), 'ctr').astype(jnp.float32)  176 us
    another operation x16, other arithmetic, solve_rows(): factor_low = jnp.linalg.cholesky(gram_matrix)  59.4 us
    another operation x11, other arithmetic, solve_rows(): lax.linalg.triangular_solve(factor_low, panel, left_side=False, lower=Tru...  49.6 us
    psum x1, waiting for transfers between devices, reduced_weights(): return lax.psum(partial_value.astype(jnp.bfloat16), 'ctr')  35.2 us
    all_gather x1, blocking collectives, local(): inner_piece = lax.all_gather(right_inner, 'row', axis=0, tiled=True)  11.3 us
    all_gather x1, blocking collectives, local(): outer_piece = lax.all_gather(right_outer, 'row', axis=0, tiled=True)  9.84 us
    another operation x5, matrix products, solve_rows(): lax.linalg.triangular_solve(factor_low, panel, left_side=False, lower=Tru...  8.67 us
  transfers between devices with their start and end apart: 6, of which 6 were waited for; matrix products, arithmetic and copies ran while one was open for 0% of the time, Pallas kernels for 0%

commit v1 on v0

--- a/solution.py
+++ b/solution.py
@@ -1,8 +1,11 @@
+import functools
 import math
 
 import jax
 import jax.numpy as jnp
 from jax import lax
+from jax.experimental import pallas as pl
+from jax.experimental.pallas import tpu as pltpu
 from jax.sharding import PartitionSpec as P
 
 STEPS = 2
@@ -33,7 +36,7 @@
     return lax.psum(partial_value.astype(jnp.bfloat16), "ctr")
 
 
-def local(left_factor, left_inner, right_inner, right_outer, pattern, start_matrix):
+def local_any(left_factor, left_inner, right_inner, right_outer, pattern, start_matrix):
     rows_here = left_factor.shape[0]
     tile_len = left_factor.shape[1]
     columns_here = left_factor.shape[2]
@@ -80,7 +83,233 @@
     return (compressed_left, weights)
 
 
+F32 = jnp.float32
+BF16 = jnp.bfloat16
+
+
+def nn(a, b):
+    return lax.dot_general(a, b, (((1,), (0,)), ((), ())), preferred_element_type=F32)
+
+
+def nt(a, b):
+    return lax.dot_general(a, b, (((1,), (1,)), ((), ())), preferred_element_type=F32)
+
+
+def inverse_factor(gram):
+    n = gram.shape[0]
+    row_at = lax.broadcasted_iota(jnp.int32, (n, n), 0)
+    col_at = lax.broadcasted_iota(jnp.int32, (n, n), 1)
+    rest = gram
+    inverse = jnp.where(row_at == col_at, 1.0, 0.0).astype(F32)
+    for j in range(n - 1):
+        ratio = rest[:, j : j + 1] / rest[j : j + 1, j : j + 1]
+        ratio = jnp.where(row_at > j, ratio, 0.0)
+        rest = rest - ratio * rest[j : j + 1, :]
+        inverse = inverse - ratio * inverse[j : j + 1, :]
+    pivots = jnp.sum(jnp.where(row_at == col_at, rest, 0.0), axis=1, keepdims=True)
+    return inverse * lax.rsqrt(pivots)
+
+
+def orth_rows(panel):
+    high = panel.astype(BF16)
+    inverse = inverse_factor(nt(high, high))
+    inverse_high = inverse.astype(BF16)
+    inverse_low = (inverse - inverse_high.astype(F32)).astype(BF16)
+    return nn(inverse_high, high) + nn(inverse_low, high)
+
+
+def kernel(
+    n_row, n_ctr, chunks,
+    u_hbm, v_hbm, x_ref, y_ref, pattern_ref, start_ref,
+    left_ref, right_ref,
+    u_all, v_all, x_all, y_all, yb_all, c_all, z_ref, couple_out, couple_in,
+    local_sem, u_send, u_recv, x_send, x_recv, yz_send, yz_recv, yr_send, yr_recv,
+    k_send, k_recv, l_send, l_recv, r_send, r_recv,
+):
+    me_r, me_c = lax.axis_index("row"), lax.axis_index("ctr")
+    tile = u_hbm.shape[1]
+    cols = u_hbm.shape[2]
+    part = x_ref.shape[0]
+    rank = start_ref.shape[0]
+    blocks = pattern_ref.shape[1]
+    step = tile // chunks
+    z_peers = [lax.rem(me_c + d, n_ctr) for d in range(n_ctr)]
+    r_peers = [lax.rem(me_r + d, n_row) for d in range(n_row)]
+    mine = pl.ds(pl.multiple_of(me_r * part, part), part)
+
+    def remote(src, dst, send, recv, where):
+        return pltpu.make_async_remote_copy(
+            src_ref=src, dst_ref=dst, send_sem=send, recv_sem=recv,
+            device_id=where, device_id_type=pl.DeviceIdType.MESH,
+        )
+
+    v_copy = pltpu.make_async_copy(v_hbm, v_all, local_sem.at[0])
+    v_copy.start()
+    own_u = pltpu.make_async_copy(u_hbm.at[me_c], u_all.at[:, pl.ds(0, cols)], local_sem.at[1])
+    own_u.start()
+
+    barrier = pltpu.get_barrier_semaphore()
+    for d in range(1, n_ctr):
+        pl.semaphore_signal(barrier, inc=1, device_id={"ctr": z_peers[d]}, device_id_type=pl.DeviceIdType.MESH)
+    for d in range(1, n_row):
+        pl.semaphore_signal(barrier, inc=1, device_id={"row": r_peers[d]}, device_id_type=pl.DeviceIdType.MESH)
+    pl.semaphore_wait(barrier, n_ctr + n_row - 2)
+
+    yz = [None] + [
+        remote(y_ref, y_all.at[mine, pl.ds(d * cols, cols)], yz_send.at[d], yz_recv.at[d], {"ctr": z_peers[d]})
+        for d in range(1, n_ctr)
+    ]
+    xs = [None] + [
+        remote(x_ref, x_all.at[mine, :], x_send.at[d], x_recv.at[d], {"row": r_peers[d]})
+        for d in range(1, n_row)
+    ]
+    for copy in yz[1:] + xs[1:]:
+        copy.start()
+    us = {}
+    for chunk in range(chunks):
+        rows = pl.ds(chunk * step, step)
+        for d in range(1, n_ctr):
+            us[chunk, d] = remote(
+                u_hbm.at[z_peers[d], rows, :], u_all.at[rows, pl.ds(d * cols, cols)],
+                u_send.at[chunk, d], u_recv.at[chunk, d], {"ctr": z_peers[d]},
+            )
+            us[chunk, d].start()
+    x_all[mine, :] = x_ref[...]
+    y_all[mine, pl.ds(0, cols)] = y_ref[...]
+    yr = {}
+    for k in range(n_ctr):
+        if k:
+            yz[k].wait_recv()
+        for d in range(1, n_row):
+            place = y_all.at[mine, pl.ds(k * cols, cols)]
+            yr[k, d] = remote(
+                place, place, yr_send.at[k, d], yr_recv.at[k, d], {"row": r_peers[d]}
+            )
+            yr[k, d].start()
+
+    row_at = lax.broadcasted_iota(jnp.int32, (cols, cols), 0)
+    col_at = lax.broadcasted_iota(jnp.int32, (cols, cols), 1)
+    diagonal = jnp.where(row_at // rank == col_at // rank, 1.0, 0.0).astype(F32)
+    fold = jnp.where(
+        lax.broadcasted_iota(jnp.int32, (rank, cols), 1) % rank
+        == lax.broadcasted_iota(jnp.int32, (rank, cols), 0), 1.0, 0.0
+    ).astype(BF16)
+    unfold = jnp.where(
+        lax.broadcasted_iota(jnp.int32, (cols, rank), 0) % rank
+        == lax.broadcasted_iota(jnp.int32, (cols, rank), 1), 1.0, 0.0
+    ).astype(BF16)
+    spread = jnp.where(
+        lax.broadcasted_iota(jnp.int32, (blocks, cols), 1) // rank
+        == lax.broadcasted_iota(jnp.int32, (blocks, cols), 0), 1.0, 0.0
+    ).astype(F32)
+    v_copy.wait()
+    for d in range(1, n_row):
+        xs[d].wait_recv()
+    x_turned = x_all[...].T
+    couples = [None]
+    for d in range(n_ctr):
+        kept = pattern_ref[pl.ds(z_peers[d], 1), :].astype(F32)
+        kept = nn(jnp.broadcast_to(kept, (8, blocks)).astype(BF16), spread.astype(BF16))[0:1, :]
+        product = nn(x_turned, v_all[z_peers[d]])
+        product = (product * diagonal * kept).astype(BF16)
+        compact = nn(fold, product).astype(BF16)
+        if d:
+            couple_out[d] = compact
+            copy = remote(couple_out.at[d], couple_in.at[d], k_send.at[d], k_recv.at[d], {"ctr": z_peers[d]})
+            copy.start()
+            couples.append(copy)
+        else:
+            couple_in[0] = compact
+
+    for k in range(n_ctr):
+        for d in range(1, n_row):
+            yr[k, d].wait_recv()
+        if k:
+            couples[k].wait_recv()
+        wide = (nn(unfold, couple_in[k]) * diagonal).astype(BF16)
+        at = pl.ds(k * cols, cols)
+        yb_all[:, at] = nn(y_all[:, at], wide).astype(BF16)
+
+    own_u.wait()
+    start = start_ref[...].astype(F32).astype(BF16)
+    for chunk in range(chunks):
+        rows = pl.ds(chunk * step, step)
+        for d in range(1, n_ctr):
+            us[chunk, d].wait_recv()
+        c_all[rows, :] = nt(u_all[rows, :], yb_all[...]).astype(BF16)
+        z_ref[:, rows] = nt(start, c_all[rows, :])
+
+    basis = orth_rows(z_ref[...])
+    for sweep_index in range(STEPS):
+        dual = orth_rows(nn(basis.astype(BF16), c_all[...]))
+        basis = orth_rows(nt(dual.astype(BF16), c_all[...]))
+
+    def share(ref, value, send, recv):
+        ref[me_c] = value
+        copies = [
+            remote(ref.at[me_c], ref.at[me_c], send.at[d], recv.at[d], {"ctr": z_peers[d]})
+            for d in range(1, n_ctr)
+        ]
+        for copy in copies:
+            copy.start()
+        return copies
+
+    left = share(left_ref, (basis * math.sqrt(tile)).astype(BF16), l_send, l_recv)
+    right = share(right_ref, nn(basis.astype(BF16), c_all[...]).astype(BF16), r_send, r_recv)
+    for copy in yz[1:] + xs[1:] + list(us.values()) + list(yr.values()) + couples[1:]:
+        copy.wait_send()
+    for copy in left + right:
+        copy.wait()
+
+
+def local_tile(n_row, n_ctr, left_factor, left_inner, right_inner, right_outer, pattern, start_matrix):
+    rows_here, tile, cols = left_factor.shape
+    rank = start_matrix.shape[1]
+    chunks = 4
+    dma = lambda *shape: pltpu.SemaphoreType.DMA(shape)
+    vmem = pl.BlockSpec(memory_space=pltpu.VMEM)
+    hbm = pl.BlockSpec(memory_space=pl.ANY)
+    width = n_ctr * cols
+    turned = jax.ShapeDtypeStruct((rows_here, rank, tile), BF16)
+    left, right = pl.pallas_call(
+        functools.partial(kernel, n_row, n_ctr, chunks),
+        out_shape=(turned, turned),
+        in_specs=[hbm, hbm, vmem, vmem, vmem, vmem],
+        out_specs=(vmem, vmem),
+        scratch_shapes=[
+            pltpu.VMEM((tile, width), BF16),
+            pltpu.VMEM((rows_here, tile, cols), BF16),
+            pltpu.VMEM((tile, cols), BF16),
+            pltpu.VMEM((tile, width), BF16),
+            pltpu.VMEM((tile, width), BF16),
+            pltpu.VMEM((tile, tile), BF16),
+            pltpu.VMEM((rank, tile), F32),
+            pltpu.VMEM((n_ctr, rank, cols), BF16),
+            pltpu.VMEM((n_ctr, rank, cols), BF16),
+            dma(2),
+            dma(chunks, n_ctr), dma(chunks, n_ctr),
+            dma(n_row), dma(n_row),
+            dma(n_ctr), dma(n_ctr),
+            dma(n_ctr, n_row), dma(n_ctr, n_row),
+            dma(n_ctr), dma(n_ctr),
+            dma(n_ctr), dma(n_ctr),
+            dma(n_ctr), dma(n_ctr),
+        ],
+        compiler_params=pltpu.CompilerParams(
+            collective_id=0, has_side_effects=True, vmem_limit_bytes=48 * 1024 * 1024
+        ),
+    )(left_factor, left_inner, right_inner, right_outer, pattern, start_matrix.T)
+    return left.transpose(0, 2, 1), right.transpose(0, 2, 1)
+
+
 def solution(mesh):
+    n_row, n_ctr = mesh.shape["row"], mesh.shape["ctr"]
+
+    def local(left_factor, *others):
+        if left_factor.shape[0] == n_ctr:
+            return local_tile(n_row, n_ctr, left_factor, *others)
+        return local_any(left_factor, *others)
+
     return jax.shard_map(
         local,
         mesh=mesh,

time: 395 us -> 103 us (0.26)
  waiting for transfers between devices: 212 us -> 0 us
  other arithmetic: 109 us -> 0 us
  Pallas kernels: 0 us -> 94 us
  matrix products: 30.5 us -> 0 us
  blocking collectives: 21.1 us -> 0 us
  between operations: 14.4 us -> 0.65 us
    psum x6 -> x0, waiting for transfers between devices: 211 us -> none  [the longest x5 176 us: reduced_basis(): lax.psum(partial_value.astype(jnp.bfloat16), 'ctr').astype(jnp.float32)]
    another operation x27 -> x0, other arithmetic: 109 us -> none  [the longest x16 59.4 us: solve_rows(): factor_low = jnp.linalg.cholesky(gram_matrix)]
    pallas_call x0 -> x1, Pallas kernels: none -> 94 us  [local_tile(): pl.pallas_call(functools.partial(kernel, n_row, n_ctr, chunks), out_shape...]
    dot_general x24 -> x0, matrix products: 21.9 us -> none  [the longest x5 6.11 us: gram_of(): jnp.einsum('itr,its->irs', panel, panel, precision=highest, preferred_ele...]
    all_gather x2 -> x0, blocking collectives: 21.1 us -> none  [the longest x1 11.3 us: local(): inner_piece = lax.all_gather(right_inner, 'row', axis=0, tiled=True)]
    another operation x5 -> x0, matrix products: 8.67 us -> none  [solve_rows(): lax.linalg.triangular_solve(factor_low, panel, left_side=False, lower=Tru...]
  transfers between devices with their start and end apart: 6 -> 0, of which waited for: 6 -> 0; matrix products, arithmetic and copies ran while one was open for 0% -> 0% of each run, Pallas kernels for 0% -> 0%
where the time goes in v1:
time: 103 us
  Pallas kernels  94 us (91%)
  local copies, waits for them, and re-layouts  7.84 us (8%)
    pallas_call x1, Pallas kernels, local_tile(): pl.pallas_call(functools.partial(kernel, n_row, n_ctr, chunks), out_shape...  94 us
    unnamed x14, local copies, waits for them, and re-layouts  7.84 us

profile of v1, /device:TPU:0, one launch (start us, length us, event | category | flops | bytes accessed | tf_op | source)
XLA Modules:
  0.0 102.5 jit_solution(1410966091433711982)
XLA Ops:
  0.6 0.0 copy-start
  0.6 1.6 %copy-done = bf16[4,1024,256]{2,1,0:T(8,128)(2,1)S(1)} copy-done((bf16[4,1024,256]{2,1,0:T(8,128)(2,1)S(1)}, bf16[4,1024,256]{2,1,0:T(8,128)(2,1)}, u32[]{:S(2)}) %copy-start) | copy-done | bytes 2097176
  2.2 0.0 copy-start.1
  2.2 1.6 %copy-done.1 = bf16[4,1024,256]{2,1,0:T(8,128)(2,1)S(1)} copy-done((bf16[4,1024,256]{2,1,0:T(8,128)(2,1)S(1)}, bf16[4,1024,256]{2,1,0:T(8,128)(2,1)}, u32[]{:S(2)}) %copy-start.1) | copy-done | bytes 2097176
  3.8 0.0 copy-start.2
  3.8 0.9 copy-done.2
  4.7 0.0 copy-start.3
  4.7 0.8 copy-done.3
  5.6 0.0 copy-start.4
  5.6 0.8 copy-done.4
  6.4 0.0 copy-start.5
  6.4 0.7 copy-done.5
  7.1 94.0 %shard_map.77 = (bf16[4,32,1024]{2,1,0:T(8,128)(2,1)S(1)}, bf16[4,32,1024]{2,1,0:T(8,128)(2,1)S(1)}) custom-call(bf16[4,1024,256]{2,1,0:T(8,128)(2,1)S(1)} %copy-done, bf16[4,1024,256]{2,1,0:T(8,128)(2,1)S(1)} %copy-done.1, bf16[128,256]{1,0:T(8,128)(2,1)S(1)} %copy-done.3, bf16[128,256]{1,0:T(8,128)(2,1)S(1)} %copy-done.4, s32[4,8]{1,0:T(4,128)S(1)} %copy-done.5, ...), custom_call_target="tpu_custom_call" | custom-call | tf_op jit(solution)/shard_map/pallas_call | solution.py:274
  101.1 0.7 copy.10
  101.8 0.7 copy.11
Async XLA Ops:
  0.6 1.6 %copy-start = (bf16[4,1024,256]{2,1,0:T(8,128)(2,1)S(1)}, bf16[4,1024,256]{2,1,0:T(8,128)(2,1)}, u32[]{:S(2)}) copy-start(bf16[4,1024,256]{2,1,0:T(8,128)(2,1)} %u_hbm.1) | copy-start | bytes 6291460
  2.2 1.6 %copy-start.1 = (bf16[4,1024,256]{2,1,0:T(8,128)(2,1)S(1)}, bf16[4,1024,256]{2,1,0:T(8,128)(2,1)}, u32[]{:S(2)}) copy-start(bf16[4,1024,256]{2,1,0:T(8,128)(2,1)} %v_hbm.1) | copy-start | bytes 6291460
  3.8 0.9 copy-start.2
  4.7 0.8 copy-start.3
  5.6 0.8 copy-start.4
  6.4 0.7 copy-start.5

commit v2 on v1

--- a/solution.py
+++ b/solution.py
@@ -101,35 +101,49 @@
     col_at = lax.broadcasted_iota(jnp.int32, (n, n), 1)
     rest = gram
     inverse = jnp.where(row_at == col_at, 1.0, 0.0).astype(F32)
-    for j in range(n - 1):
-        ratio = rest[:, j : j + 1] / rest[j : j + 1, j : j + 1]
-        ratio = jnp.where(row_at > j, ratio, 0.0)
-        rest = rest - ratio * rest[j : j + 1, :]
-        inverse = inverse - ratio * inverse[j : j + 1, :]
-    pivots = jnp.sum(jnp.where(row_at == col_at, rest, 0.0), axis=1, keepdims=True)
-    return inverse * lax.rsqrt(pivots)
-
-
-def orth_rows(panel):
-    high = panel.astype(BF16)
-    inverse = inverse_factor(nt(high, high))
-    inverse_high = inverse.astype(BF16)
-    inverse_low = (inverse - inverse_high.astype(F32)).astype(BF16)
+    scale = jnp.zeros_like(gram)
+    for first in range(0, n, 8):
+        last = min(first + 8, n)
+        panel = {j: jnp.broadcast_to(rest[:, j : j + 1], (n, n)) for j in range(first, last)}
+        for j in range(first, last):
+            pivot = panel[j][j : j + 1, :]
+            scale = jnp.where(row_at == j, lax.rsqrt(pivot), scale)
+            ratio = jnp.where(row_at > j, panel[j] * (1.0 / pivot), 0.0)
+            for m in range(j + 1, last):
+                panel[m] = panel[m] - ratio * panel[m][j : j + 1, :]
+            rest = rest - ratio * rest[j : j + 1, :]
+            inverse = inverse - ratio * inverse[j : j + 1, :]
+    return inverse * scale
+
+
+def split(value):
+    high = value.astype(BF16)
+    return high, (value - high.astype(F32)).astype(BF16)
+
+
+def apply_to(inverse, high):
+    inverse_high, inverse_low = split(inverse)
     return nn(inverse_high, high) + nn(inverse_low, high)
+
+
+def apply_wide(inverse, value):
+    inverse_high, inverse_low = split(inverse)
+    high, low = split(value)
+    return nn(inverse_high, high) + nn(inverse_low, high) + nn(inverse_high, low)
 
 
 def kernel(
     n_row, n_ctr, chunks,
-    u_hbm, v_hbm, x_ref, y_ref, pattern_ref, start_ref,
+    u_hbm, v_hbm, x_hbm, y_hbm, pattern_hbm, start_hbm,
     left_ref, right_ref,
-    u_all, v_all, x_all, y_all, yb_all, c_all, z_ref, couple_out, couple_in,
+    u_all, v_all, x_all, y_all, yb_all, c_all, z_ref, couple_out, couple_in, pattern_ref, start_ref, panels_ref, inverses_ref,
     local_sem, u_send, u_recv, x_send, x_recv, yz_send, yz_recv, yr_send, yr_recv,
-    k_send, k_recv, l_send, l_recv, r_send, r_recv,
+    k_send, k_recv, l_send, l_recv, r_send, r_recv, i_send, i_recv,
 ):
     me_r, me_c = lax.axis_index("row"), lax.axis_index("ctr")
     tile = u_hbm.shape[1]
     cols = u_hbm.shape[2]
-    part = x_ref.shape[0]
+    part = x_hbm.shape[0]
     rank = start_ref.shape[0]
     blocks = pattern_ref.shape[1]
     step = tile // chunks
@@ -147,6 +161,12 @@
     v_copy.start()
     own_u = pltpu.make_async_copy(u_hbm.at[me_c], u_all.at[:, pl.ds(0, cols)], local_sem.at[1])
     own_u.start()
+    own_x = pltpu.make_async_copy(x_hbm, x_all.at[mine, :], local_sem.at[2])
+    own_y = pltpu.make_async_copy(y_hbm, y_all.at[mine, pl.ds(0, cols)], local_sem.at[3])
+    get_pattern = pltpu.make_async_copy(pattern_hbm, pattern_ref, local_sem.at[4])
+    get_start = pltpu.make_async_copy(start_hbm, start_ref, local_sem.at[5])
+    for copy in (own_x, own_y, get_pattern, get_start):
+        copy.start()
 
     barrier = pltpu.get_barrier_semaphore()
     for d in range(1, n_ctr):
@@ -156,11 +176,11 @@
     pl.semaphore_wait(barrier, n_ctr + n_row - 2)
 
     yz = [None] + [
-        remote(y_ref, y_all.at[mine, pl.ds(d * cols, cols)], yz_send.at[d], yz_recv.at[d], {"ctr": z_peers[d]})
+        remote(y_hbm, y_all.at[mine, pl.ds(d * cols, cols)], yz_send.at[d], yz_recv.at[d], {"ctr": z_peers[d]})
         for d in range(1, n_ctr)
     ]
     xs = [None] + [
-        remote(x_ref, x_all.at[mine, :], x_send.at[d], x_recv.at[d], {"row": r_peers[d]})
+        remote(x_hbm, x_all.at[mine, :], x_send.at[d], x_recv.at[d], {"row": r_peers[d]})
         for d in range(1, n_row)
     ]
     for copy in yz[1:] + xs[1:]:
@@ -174,8 +194,7 @@
                 u_send.at[chunk, d], u_recv.at[chunk, d], {"ctr": z_peers[d]},
             )
             us[chunk, d].start()
-    x_all[mine, :] = x_ref[...]
-    y_all[mine, pl.ds(0, cols)] = y_ref[...]
+    own_y.wait()
     yr = {}
     for k in range(n_ctr):
         if k:
@@ -203,6 +222,9 @@
         == lax.broadcasted_iota(jnp.int32, (blocks, cols), 0), 1.0, 0.0
     ).astype(F32)
     v_copy.wait()
+    own_x.wait()
+    get_pattern.wait()
+    get_start.wait()
     for d in range(1, n_row):
         xs[d].wait_recv()
     x_turned = x_all[...].T
@@ -239,13 +261,14 @@
         c_all[rows, :] = nt(u_all[rows, :], yb_all[...]).astype(BF16)
         z_ref[:, rows] = nt(start, c_all[rows, :])
 
-    basis = orth_rows(z_ref[...])
+    panel = z_ref[...].astype(BF16)
     for sweep_index in range(STEPS):
-        dual = orth_rows(nn(basis.astype(BF16), c_all[...]))
-        basis = orth_rows(nt(dual.astype(BF16), c_all[...]))
-
-    def share(ref, value, send, recv):
-        ref[me_c] = value
+        inverse = inverse_factor(nt(panel, panel))
+        panel = apply_wide(inverse, nn(panel, c_all[...])).astype(BF16)
+        inverse = inverse_factor(nt(panel, panel))
+        panel = apply_wide(inverse, nt(panel, c_all[...])).astype(BF16)
+
+    def share(ref, send, recv):
         copies = [
             remote(ref.at[me_c], ref.at[me_c], send.at[d], recv.at[d], {"ctr": z_peers[d]})
             for d in range(1, n_ctr)
@@ -254,12 +277,26 @@
             copy.start()
         return copies
 
-    left = share(left_ref, (basis * math.sqrt(tile)).astype(BF16), l_send, l_recv)
-    right = share(right_ref, nn(basis.astype(BF16), c_all[...]).astype(BF16), r_send, r_recv)
+    panels_ref[me_c] = panel
+    panel_copies = share(panels_ref, l_send, l_recv)
+    inverse = inverse_factor(nt(panel, panel))
+    inverses_ref[me_c] = inverse
+    inverse_copies = share(inverses_ref, i_send, i_recv)
+    right_ref[me_c] = apply_wide(inverse, nn(panel, c_all[...])).astype(BF16)
+    right_copies = share(right_ref, r_send, r_recv)
+    for d in range(n_ctr):
+        if d:
+            panel_copies[d - 1].wait_recv()
+            inverse_copies[d - 1].wait_recv()
+        source = lax.rem(me_c + (n_ctr - d), n_ctr)
+        basis = apply_to(inverses_ref[source], panels_ref[source])
+        left_ref[source] = (basis * math.sqrt(tile)).astype(BF16)
+    for copy in right_copies:
+        copy.wait_recv()
+    for copy in panel_copies + inverse_copies + right_copies:
+        copy.wait_send()
     for copy in yz[1:] + xs[1:] + list(us.values()) + list(yr.values()) + couples[1:]:
         copy.wait_send()
-    for copy in left + right:
-        copy.wait()
 
 
 def local_tile(n_row, n_ctr, left_factor, left_inner, right_inner, right_outer, pattern, start_matrix):
@@ -274,7 +311,7 @@
     left, right = pl.pallas_call(
         functools.partial(kernel, n_row, n_ctr, chunks),
         out_shape=(turned, turned),
-        in_specs=[hbm, hbm, vmem, vmem, vmem, vmem],
+        in_specs=[hbm] * 6,
         out_specs=(vmem, vmem),
         scratch_shapes=[
             pltpu.VMEM((tile, width), BF16),
@@ -286,7 +323,11 @@
             pltpu.VMEM((rank, tile), F32),
             pltpu.VMEM((n_ctr, rank, cols), BF16),
             pltpu.VMEM((n_ctr, rank, cols), BF16),
-            dma(2),
+            pltpu.VMEM(pattern.shape, pattern.dtype),
+            pltpu.VMEM((rank, tile), start_matrix.dtype),
+            pltpu.VMEM((n_ctr, rank, tile), BF16),
+            pltpu.VMEM((n_ctr, rank, rank), F32),
+            dma(6),
             dma(chunks, n_ctr), dma(chunks, n_ctr),
             dma(n_row), dma(n_row),
             dma(n_ctr), dma(n_ctr),
@@ -294,9 +335,10 @@
             dma(n_ctr), dma(n_ctr),
             dma(n_ctr), dma(n_ctr),
             dma(n_ctr), dma(n_ctr),
+            dma(n_ctr), dma(n_ctr),
         ],
         compiler_params=pltpu.CompilerParams(
-            collective_id=0, has_side_effects=True, vmem_limit_bytes=48 * 1024 * 1024
+            collective_id=0, has_side_effects=True, vmem_limit_bytes=62 * 1024 * 1024
         ),
     )(left_factor, left_inner, right_inner, right_outer, pattern, start_matrix.T)
     return left.transpose(0, 2, 1), right.transpose(0, 2, 1)

time: 103 us -> 89.3 us (0.87)
  Pallas kernels: 94 us -> 85.1 us
  local copies, waits for them, and re-layouts: 7.84 us -> 3.34 us
    pallas_call x1, Pallas kernels: 94 us -> 85.1 us  [local_tile(): pl.pallas_call(functools.partial(kernel, n_row, n_ctr, chunks), out_shape...]
    unnamed x14 -> x2, local copies, waits for them, and re-layouts: 7.84 us -> 3.34 us
where the time goes in v2:
time: 89.3 us; the launch traced here: 89.1 us
  Pallas kernels  85.1 us (95%)
  local copies, waits for them, and re-layouts  3.34 us (4%)
    pallas_call x1, Pallas kernels, local_tile(): pl.pallas_call(functools.partial(kernel, n_row, n_ctr, chunks), out_shape...  85.1 us
    unnamed x2, local copies, waits for them, and re-layouts  3.34 us

profile of v2, /device:TPU:0, one launch (start us, length us, event | category | flops | bytes accessed | tf_op | source)
XLA Modules:
  0.0 89.1 jit_solution(5236851018303697818)
XLA Ops:
  0.6 85.1 %shard_map.77 = (bf16[4,32,1024]{2,1,0:T(8,128)(2,1)}, bf16[4,32,1024]{2,1,0:T(8,128)(2,1)}) custom-call(bf16[4,1024,256]{2,1,0:T(8,128)(2,1)} %u_hbm.1, bf16[4,1024,256]{2,1,0:T(8,128)(2,1)} %v_hbm.1, bf16[128,256]{1,0:T(8,128)(2,1)} %x_hbm.1, bf16[128,256]{1,0:T(8,128)(2,1)} %y_hbm.1, s32[4,8]{1,0:T(4,128)} %pattern_hbm.1, s32[32,1024]{1,0:T(8,128)} %bitcast.5), custom_call_target="tpu_custom_call" | custom-call | tf_op jit(solution)/shard_map/pallas_call | solution.py:311
  85.8 1.7 %copy.10 = bf16[4,1024,32]{1,2,0:T(8,128)(2,1)} copy(bf16[4,1024,32]{1,2,0:T(8,128)(2,1)} %bitcast.4) | data formatting | bytes 524288
  87.4 1.7 %copy.11 = bf16[4,1024,32]{1,2,0:T(8,128)(2,1)} copy(bf16[4,1024,32]{1,2,0:T(8,128)(2,1)} %bitcast.3) | data formatting | bytes 524288

commit v3 on v2

--- a/solution.py
+++ b/solution.py
@@ -136,9 +136,9 @@
     n_row, n_ctr, chunks,
     u_hbm, v_hbm, x_hbm, y_hbm, pattern_hbm, start_hbm,
     left_ref, right_ref,
-    u_all, v_all, x_all, y_all, yb_all, c_all, z_ref, couple_out, couple_in, pattern_ref, start_ref, panels_ref, inverses_ref,
+    u_all, v_all, x_all, y_all, yb_all, c_all, z_ref, couple_out, couple_in, pattern_ref, start_ref,
     local_sem, u_send, u_recv, x_send, x_recv, yz_send, yz_recv, yr_send, yr_recv,
-    k_send, k_recv, l_send, l_recv, r_send, r_recv, i_send, i_recv,
+    k_send, k_recv, l_send, l_recv, r_send, r_recv,
 ):
     me_r, me_c = lax.axis_index("row"), lax.axis_index("ctr")
     tile = u_hbm.shape[1]
@@ -174,6 +174,17 @@
     for d in range(1, n_row):
         pl.semaphore_signal(barrier, inc=1, device_id={"row": r_peers[d]}, device_id_type=pl.DeviceIdType.MESH)
     pl.semaphore_wait(barrier, n_ctr + n_row - 2)
+
+    def slot(at):
+        return y_all.at[mine, pl.ds(at * cols, cols)]
+
+    def hop_right(src, dst, send, recv, d):
+        return remote(src, dst, send.at[0, d], recv.at[0, d + 1], {"ctr": me_c + 1})
+
+    def hop_left(src, dst, send, recv, d):
+        return remote(src, dst, send.at[1, d], recv.at[1, d + 1], {"ctr": me_c - 1})
+
+    has_right, has_left = me_c + 1 < n_ctr, me_c > 0
 
     yz = [None] + [
         remote(y_hbm, y_all.at[mine, pl.ds(d * cols, cols)], yz_send.at[d], yz_recv.at[d], {"ctr": z_peers[d]})
@@ -195,16 +206,20 @@
             )
             us[chunk, d].start()
     own_y.wait()
-    yr = {}
+    yr = {
+        (k, d): remote(slot(k), slot(k), yr_send.at[k, d], yr_recv.at[k, d], {"row": r_peers[d]})
+        for k in range(n_ctr)
+        for d in range(1, n_row)
+    }
+
+    def to_rows(k):
+        for d in range(1, n_row):
+            yr[k, d].start()
+
     for k in range(n_ctr):
         if k:
             yz[k].wait_recv()
-        for d in range(1, n_row):
-            place = y_all.at[mine, pl.ds(k * cols, cols)]
-            yr[k, d] = remote(
-                place, place, yr_send.at[k, d], yr_recv.at[k, d], {"row": r_peers[d]}
-            )
-            yr[k, d].start()
+        to_rows(k)
 
     row_at = lax.broadcasted_iota(jnp.int32, (cols, cols), 0)
     col_at = lax.broadcasted_iota(jnp.int32, (cols, cols), 1)
@@ -268,33 +283,51 @@
         inverse = inverse_factor(nt(panel, panel))
         panel = apply_wide(inverse, nt(panel, c_all[...])).astype(BF16)
 
-    def share(ref, send, recv):
-        copies = [
-            remote(ref.at[me_c], ref.at[me_c], send.at[d], recv.at[d], {"ctr": z_peers[d]})
-            for d in range(1, n_ctr)
-        ]
-        for copy in copies:
-            copy.start()
-        return copies
-
-    panels_ref[me_c] = panel
-    panel_copies = share(panels_ref, l_send, l_recv)
+    def out_right(ref, send, recv, d):
+        at = ref.at[me_c - d]
+        return hop_right(at, at, send, recv, d)
+
+    def out_left(ref, send, recv, d):
+        at = ref.at[me_c + d]
+        return hop_left(at, at, send, recv, d)
+
+    def begin(out):
+        pl.when(has_right)(lambda: out_right(*out, 0).start())
+        pl.when(has_left)(lambda: out_left(*out, 0).start())
+
+    outs = [(left_ref, l_send, l_recv), (right_ref, r_send, r_recv)]
     inverse = inverse_factor(nt(panel, panel))
-    inverses_ref[me_c] = inverse
-    inverse_copies = share(inverses_ref, i_send, i_recv)
+    left_ref[me_c] = (apply_to(inverse, panel) * math.sqrt(tile)).astype(BF16)
+    begin(outs[0])
     right_ref[me_c] = apply_wide(inverse, nn(panel, c_all[...])).astype(BF16)
-    right_copies = share(right_ref, r_send, r_recv)
-    for d in range(n_ctr):
-        if d:
-            panel_copies[d - 1].wait_recv()
-            inverse_copies[d - 1].wait_recv()
-        source = lax.rem(me_c + (n_ctr - d), n_ctr)
-        basis = apply_to(inverses_ref[source], panels_ref[source])
-        left_ref[source] = (basis * math.sqrt(tile)).astype(BF16)
-    for copy in right_copies:
-        copy.wait_recv()
-    for copy in panel_copies + inverse_copies + right_copies:
-        copy.wait_send()
+    begin(outs[1])
+    for d in range(1, n_ctr):
+        for out in outs:
+
+            @pl.when(me_c >= d)
+            def _():
+                hop_right(out[0].at[me_c - d], out[0].at[me_c - d], out[1], out[2], d - 1).wait_recv()
+                if d + 1 < n_ctr:
+                    pl.when(has_right)(lambda: out_right(*out, d).start())
+
+            @pl.when(me_c + d < n_ctr)
+            def _():
+                hop_left(out[0].at[me_c + d], out[0].at[me_c + d], out[1], out[2], d - 1).wait_recv()
+                if d + 1 < n_ctr:
+                    pl.when(has_left)(lambda: out_left(*out, d).start())
+
+    for d in range(n_ctr - 1):
+
+        @pl.when(jnp.logical_and(has_right, me_c >= d))
+        def _():
+            for out in outs:
+                out_right(*out, d).wait_send()
+
+        @pl.when(jnp.logical_and(has_left, me_c + d < n_ctr))
+        def _():
+            for out in outs:
+                out_left(*out, d).wait_send()
+
     for copy in yz[1:] + xs[1:] + list(us.values()) + list(yr.values()) + couples[1:]:
         copy.wait_send()
 
@@ -302,7 +335,7 @@
 def local_tile(n_row, n_ctr, left_factor, left_inner, right_inner, right_outer, pattern, start_matrix):
     rows_here, tile, cols = left_factor.shape
     rank = start_matrix.shape[1]
-    chunks = 4
+    chunks = 2
     dma = lambda *shape: pltpu.SemaphoreType.DMA(shape)
     vmem = pl.BlockSpec(memory_space=pltpu.VMEM)
     hbm = pl.BlockSpec(memory_space=pl.ANY)
@@ -325,17 +358,14 @@
             pltpu.VMEM((n_ctr, rank, cols), BF16),
             pltpu.VMEM(pattern.shape, pattern.dtype),
             pltpu.VMEM((rank, tile), start_matrix.dtype),
-            pltpu.VMEM((n_ctr, rank, tile), BF16),
-            pltpu.VMEM((n_ctr, rank, rank), F32),
             dma(6),
             dma(chunks, n_ctr), dma(chunks, n_ctr),
             dma(n_row), dma(n_row),
             dma(n_ctr), dma(n_ctr),
             dma(n_ctr, n_row), dma(n_ctr, n_row),
             dma(n_ctr), dma(n_ctr),
-            dma(n_ctr), dma(n_ctr),
-            dma(n_ctr), dma(n_ctr),
-            dma(n_ctr), dma(n_ctr),
+            dma(2, n_ctr), dma(2, n_ctr),
+            dma(2, n_ctr), dma(2, n_ctr),
         ],
         compiler_params=pltpu.CompilerParams(
             collective_id=0, has_side_effects=True, vmem_limit_bytes=62 * 1024 * 1024

time: 89.3 us -> 86.1 us (0.964)
  Pallas kernels: 85.1 us -> 81.9 us
    pallas_call x1, Pallas kernels: 85.1 us -> 81.9 us  [local_tile(): pl.pallas_call(functools.partial(kernel, n_row, n_ctr, chunks), out_shape...]
where the time goes in v3:
time: 86.1 us; the launch traced here: 85.9 us
  Pallas kernels  81.9 us (95%)
  local copies, waits for them, and re-layouts  3.34 us (4%)
    pallas_call x1, Pallas kernels, local_tile(): pl.pallas_call(functools.partial(kernel, n_row, n_ctr, chunks), out_shape...  81.9 us
    unnamed x2, local copies, waits for them, and re-layouts  3.34 us

profile of v3, /device:TPU:0, one launch (start us, length us, event | category | flops | bytes accessed | tf_op | source)
XLA Modules:
  0.0 85.9 jit_solution(7373231444394644852)
XLA Ops:
  0.6 81.9 %shard_map.77 = (bf16[4,32,1024]{2,1,0:T(8,128)(2,1)}, bf16[4,32,1024]{2,1,0:T(8,128)(2,1)}) custom-call(bf16[4,1024,256]{2,1,0:T(8,128)(2,1)} %u_hbm.1, bf16[4,1024,256]{2,1,0:T(8,128)(2,1)} %v_hbm.1, bf16[128,256]{1,0:T(8,128)(2,1)} %x_hbm.1, bf16[128,256]{1,0:T(8,128)(2,1)} %y_hbm.1, s32[4,8]{1,0:T(4,128)} %pattern_hbm.1, s32[32,1024]{1,0:T(8,128)} %bitcast.5), custom_call_target="tpu_custom_call" | custom-call | tf_op jit(solution)/shard_map/pallas_call | solution.py:344
  82.5 1.7 %copy.10 = bf16[4,1024,32]{1,2,0:T(8,128)(2,1)} copy(bf16[4,1024,32]{1,2,0:T(8,128)(2,1)} %bitcast.4) | data formatting | bytes 524288
  84.2 1.7 %copy.11 = bf16[4,1024,32]{1,2,0:T(8,128)(2,1)} copy(bf16[4,1024,32]{1,2,0:T(8,128)(2,1)} %bitcast.3) | data formatting | bytes 524288

commit v4 on v3

--- a/solution.py
+++ b/solution.py
@@ -204,7 +204,8 @@
                 u_hbm.at[z_peers[d], rows, :], u_all.at[rows, pl.ds(d * cols, cols)],
                 u_send.at[chunk, d], u_recv.at[chunk, d], {"ctr": z_peers[d]},
             )
-            us[chunk, d].start()
+            if chunk == 0:
+                us[chunk, d].start()
     own_y.wait()
     yr = {
         (k, d): remote(slot(k), slot(k), yr_send.at[k, d], yr_recv.at[k, d], {"row": r_peers[d]})
@@ -258,6 +259,10 @@
         else:
             couple_in[0] = compact
 
+    for chunk in range(1, chunks):
+        for d in range(1, n_ctr):
+            us[chunk, d].start()
+
     for k in range(n_ctr):
         for d in range(1, n_row):
             yr[k, d].wait_recv()
@@ -335,7 +340,7 @@
 def local_tile(n_row, n_ctr, left_factor, left_inner, right_inner, right_outer, pattern, start_matrix):
     rows_here, tile, cols = left_factor.shape
     rank = start_matrix.shape[1]
-    chunks = 2
+    chunks = 4
     dma = lambda *shape: pltpu.SemaphoreType.DMA(shape)
     vmem = pl.BlockSpec(memory_space=pltpu.VMEM)
     hbm = pl.BlockSpec(memory_space=pl.ANY)

time: 86.1 us -> 84.3 us (0.979)
  Pallas kernels: 81.9 us -> 80.1 us
    pallas_call x1, Pallas kernels: 81.9 us -> 80.1 us  [local_tile(): pl.pallas_call(functools.partial(kernel, n_row, n_ctr, chunks), out_shape...]
where the time goes in v4:
time: 84.3 us; the launch traced here: 84.1 us
  Pallas kernels  80.1 us (95%)
  local copies, waits for them, and re-layouts  3.34 us (4%)
    pallas_call x1, Pallas kernels, local_tile(): pl.pallas_call(functools.partial(kernel, n_row, n_ctr, chunks), out_shape...  80.1 us
    unnamed x2, local copies, waits for them, and re-layouts  3.34 us

profile of v4, /device:TPU:0, one launch (start us, length us, event | category | flops | bytes accessed | tf_op | source)
XLA Modules:
  0.0 84.1 jit_solution(9369466204722435156)
XLA Ops:
  0.6 80.1 %shard_map.77 = (bf16[4,32,1024]{2,1,0:T(8,128)(2,1)}, bf16[4,32,1024]{2,1,0:T(8,128)(2,1)}) custom-call(bf16[4,1024,256]{2,1,0:T(8,128)(2,1)} %u_hbm.1, bf16[4,1024,256]{2,1,0:T(8,128)(2,1)} %v_hbm.1, bf16[128,256]{1,0:T(8,128)(2,1)} %x_hbm.1, bf16[128,256]{1,0:T(8,128)(2,1)} %y_hbm.1, s32[4,8]{1,0:T(4,128)} %pattern_hbm.1, s32[32,1024]{1,0:T(8,128)} %bitcast.5), custom_call_target="tpu_custom_call" | custom-call | tf_op jit(solution)/shard_map/pallas_call | solution.py:349
  80.8 1.7 %copy.10 = bf16[4,1024,32]{1,2,0:T(8,128)(2,1)} copy(bf16[4,1024,32]{1,2,0:T(8,128)(2,1)} %bitcast.4) | data formatting | bytes 524288
  82.5 1.7 %copy.11 = bf16[4,1024,32]{1,2,0:T(8,128)(2,1)} copy(bf16[4,1024,32]{1,2,0:T(8,128)(2,1)} %bitcast.3) | data formatting | bytes 524288
